TPU v7x, 32 devices: a whole 2x2x4 slice. The times are simulated.
32 devices in a mesh: gx: 8 (over y, x, core), gy: 4 (over z).
Axes of the slice: x: 2, y: 2, z: 4, core: 2. Of those that a mesh axis runs over, the one named last changes fastest.
Arguments:
- density: float32 [512, 2048], P('gx', 'gy'), may hold values from 0.5 to 4
- energy: float32 [512, 2048], P('gx', 'gy'), may hold values from 0.5 to 3
- displacement: float32 [2, 512, 2048], P(None, 'gx', 'gy'), may hold values from -0.4 to 0.4
- tile_mat: int32 [512, 16], P('gx', 'gy'), may hold values from 0 to 3
- store_frac: float32 [1024, 128], P(('gx', 'gy')), may hold values from 0.05 to 0.95
- store_state: float32 [2, 1024, 128], P(None, ('gx', 'gy')), may hold values from 0.5 to 4
- store_route: int32 [3, 1024], P(None, ('gx', 'gy')), may hold values from 0 to 255, as said below
Outputs:
- remapped: float32 [4, 3, 512, 2048], P(None, None, 'gx', 'gy')
- totals: float32 [2, 4], replicated
Inputs may be any that keep to these rules, and one draw needn't show every extreme that they name: `store_route`: row 0 is an index along gy; among the stored tiles of one device at most 16 have the same row-0 value, and in every draw some device reaches 16 for some value. Row 1 is a tile index of 0 to 255; stored tiles with the same receiving device (same gx block row, same row-0 value) name distinct tiles. Row 2 is a material of 0 to 3 that differs from tile_mat of the named tile.
All inputs are finite; a program needn't handle non-finite values.
Results may differ from a plain program's by a relative error of at most 0.0003.
Values sent between devices are 32-bit elements; how exact they have to be, the bound alone decides.
A program may use at most 64 MiB of HBM per device.

v0:
```python
import jax
import jax.numpy as jnp
from jax import lax
from jax.sharding import PartitionSpec as P

M = 4
TILE = 128


def passed_along(value, axis, steps):
    count = lax.axis_size(axis)
    first, last = (max(0, -steps), min(count, count - steps))
    return lax.ppermute(value, axis, [(source, source + steps) for source in range(first, last)])


def padded_2(shard, sides, width):
    for axis, dim in sides:
        size, length = (lax.axis_size(axis), shard.shape[dim])
        up = [(i, (i + 1) % size) for i in range(size - 1)]
        down = [(j, i) for i, j in up]
        last = lax.slice_in_dim(shard, length - width, length, axis=dim)
        first = lax.slice_in_dim(shard, 0, width, axis=dim)
        before = lax.ppermute(last, axis, up)
        after = lax.ppermute(first, axis, down)
        shard = jnp.concatenate([before, shard, after], axis=dim)
    return shard


def slopes(padded):
    across_sum = padded[..., :, :-2] + padded[..., :, 1:-1] + padded[..., :, 2:]
    slope_x = (across_sum[..., 2:, :] - across_sum[..., :-2, :]) / 6.0
    along_sum = padded[..., :-2, :] + padded[..., 1:-1, :] + padded[..., 2:, :]
    slope_y = (along_sum[..., :, 2:] - along_sum[..., :, :-2]) / 6.0
    return (slope_x, slope_y)


def upwind(face_speed, lower_side, upper_side):
    return face_speed * 0.5 * (lower_side + upper_side) - 0.5 * jnp.abs(face_speed) * (
        upper_side - lower_side
    )


def advance(extended, slope_x, slope_y, x_speed, y_speed):
    lower_side = extended[..., :-1, 1:-1] + 0.5 * slope_x[..., :-1, 1:-1]
    upper_side = extended[..., 1:, 1:-1] - 0.5 * slope_x[..., 1:, 1:-1]
    x_flux = upwind(x_speed, lower_side, upper_side)
    left_side = extended[..., 1:-1, :-1] + 0.5 * slope_y[..., 1:-1, :-1]
    right_side = extended[..., 1:-1, 1:] - 0.5 * slope_y[..., 1:-1, 1:]
    y_flux = upwind(y_speed, left_side, right_side)
    interior = extended[..., 1:-1, 1:-1]
    return (
        interior
        + x_flux[..., :-1, :]
        - x_flux[..., 1:, :]
        + y_flux[..., :, :-1]
        - y_flux[..., :, 1:]
    )


def speeds(node_disp, x_open, y_open):
    x_speed = -0.5 * (node_disp[0, :, :-1] + node_disp[0, :, 1:])
    y_speed = -0.5 * (node_disp[1, :-1, :] + node_disp[1, 1:, :])
    return (x_speed * x_open[:, None], y_speed * y_open[None, :])


def conserved(primary, second, mixed_data, density, energy, material):
    own_part = (primary == material).astype(jnp.float32) * (1.0 - mixed_data[0])
    other_part = (second == material).astype(jnp.float32) * mixed_data[0]
    volume = own_part + other_part
    mass = own_part * density + other_part * mixed_data[1]
    energy_total = own_part * density * energy + other_part * mixed_data[1] * mixed_data[2]
    return jnp.stack([volume, mass, energy_total])


def open_faces(cell_count, axis_index, axis_count):
    face_index = jnp.arange(cell_count + 1, dtype=jnp.int32)
    closed = (face_index == 0) & (axis_index == 0) | (face_index == cell_count) & (
        axis_index == axis_count - 1
    )
    return jnp.where(closed, 0.0, 1.0).astype(jnp.float32)


def local(density, energy, displacement, tile_mat, store_frac, store_state, store_route):
    height_cells, width_cells = density.shape
    per_row = width_cells // TILE
    tile_count = height_cells * per_row
    cap_slots = tile_count // 16
    gy_count = lax.axis_size("gy")
    payload = jnp.stack([store_frac, store_state[0], store_state[1]], 1)
    target_gy = store_route[0]
    onehot = (target_gy[:, None] == jnp.arange(gy_count, dtype=jnp.int32)[None, :]).astype(
        jnp.int32
    )
    position = jnp.sum((jnp.cumsum(onehot, 0) - onehot) * onehot, 1)
    outgoing = (
        jnp.zeros((gy_count, cap_slots, 3, TILE), jnp.float32).at[target_gy, position].set(payload)
    )
    labels = jnp.stack([store_route[1], store_route[2]], 1).astype(jnp.float32)
    outgoing_labels = (
        jnp.full((gy_count, cap_slots, 2), -1.0, jnp.float32).at[target_gy, position].set(labels)
    )
    arrived, arrived_labels = (
        lax.all_to_all(outgoing, "gy", split_axis=0, concat_axis=0, tiled=True),
        lax.all_to_all(outgoing_labels, "gy", split_axis=0, concat_axis=0, tiled=True),
    )
    arrived = arrived.reshape(gy_count * cap_slots, 3, TILE)
    arrived_labels = arrived_labels.reshape(gy_count * cap_slots, 2)
    target_tile = arrived_labels[:, 0].astype(jnp.int32)
    target_tile = jnp.where(target_tile < 0, tile_count, target_tile)
    material_in = arrived_labels[:, 1].astype(jnp.int32)
    mixed_data = jnp.zeros((3, tile_count, TILE), jnp.float32)
    mixed_data = mixed_data.at[:, target_tile].set(jnp.transpose(arrived, (1, 0, 2)), mode="drop")
    mixed_data = mixed_data.reshape(3, height_cells, width_cells)
    second = jnp.full((tile_count,), -1, jnp.int32).at[target_tile].set(material_in, mode="drop")
    second = jnp.repeat(second.reshape(height_cells, per_row), TILE, axis=1)
    primary = jnp.repeat(tile_mat, TILE, axis=1)
    next_rows = passed_along(displacement[:, :1, :], "gx", -1)
    node_disp = jnp.concatenate([displacement, next_rows], 1)
    next_columns = passed_along(node_disp[:, :, :1], "gy", -1)
    node_disp = jnp.concatenate([node_disp, next_columns], 2)
    x_open = open_faces(height_cells, lax.axis_index("gx"), lax.axis_size("gx"))
    y_open = open_faces(width_cells, lax.axis_index("gy"), gy_count)
    x_speed, y_speed = speeds(node_disp, x_open, y_open)
    depth = 2
    fields = jnp.concatenate(
        [conserved(primary, second, mixed_data, density, energy, material) for material in range(M)]
    )
    halo_fields = padded_2(fields, (("gx", 1), ("gy", 2)), depth)
    slope_x, slope_y = slopes(halo_fields)
    extended = halo_fields[:, 1:-1, 1:-1]
    remapped = advance(extended, slope_x, slope_y, x_speed, y_speed).reshape(
        M, 3, height_cells, width_cells
    )
    totals = lax.psum(jnp.sum(remapped[:, 1:], axis=(2, 3)).T, ("gx", "gy"))
    return (remapped, totals)


def solution(mesh):
    placed = (
        P("gx", "gy"),
        P("gx", "gy"),
        P(None, "gx", "gy"),
        P("gx", "gy"),
        P(("gx", "gy"), None),
        P(None, ("gx", "gy"), None),
        P(None, ("gx", "gy")),
    )
    return jax.shard_map(
        local,
        mesh=mesh,
        in_specs=placed,
        out_specs=(P(None, None, "gx", "gy"), P()),
        check_vma=False,
    )
```

profile of v0, /device:TPU:0, one launch (start us, length us, event | category | flops | bytes accessed | tf_op | source)
XLA Modules:
  0.0 112.7 jit_solution(10318267996030565868)
XLA Ops:
  0.6 0.8 slice_bitcast_fusion.3
  1.4 0.1 fusion.13
  1.6 0.2 select_reduce_fusion
  1.7 0.7 fusion.22
  2.4 0.1 copy.31
  2.5 2.2 %scatter_fusion = f32[4,16,2]{2,1,0:T(8,128)S(1)} fusion(f32[4,16,2]{2,1,0:T(8,128)S(1)} %broadcast_in_dim.65, s32[32]{0:T(128)S(1)} %fusion.22, f32[32,2]{1,0:T(8,128)S(1)} %copy.31), kind=kCustom, calls=%fused_computation | custom fusion | bytes 1024 | tf_op jit(solution)/shard_map/scatter | solution.py:100
  4.7 0.7 copy.32
  5.4 6.3 %all-to-all-start = ((f32[4,16,2]{1,2,0:T(2,128)}), f32[4,16,2]{1,2,0:T(2,128)S(1)}, u32[]{:S(2)}, u32[]{:S(2)}) async-start(f32[4,16,2]{1,2,0:T(2,128)} %copy.32), calls=%async_computation | async-start | bytes 8192 | tf_op jit(solution)/shard_map/all_to_all | solution.py:104
  11.7 0.8 slice.171
  12.5 1.3 %collective-permute-start = (f32[2,1,512]{2,1,0:T(1,128)S(1)}, f32[2,1,512]{2,1,0:T(1,128)S(1)}, u32[]{:S(2)}, u32[]{:S(2)}) collective-permute-start(f32[2,1,512]{2,1,0:T(1,128)S(1)} %slice.171), channel_id=1, source_target_pairs={{4,0},{8,4},{12,8},{16,12},{20,16},{24,20},{28,24},{5,1},{9,5},{13... | collective-permute-start | bytes 12296 | tf_op jit(solution)/shard_map/ppermute | solution.py:13
  13.8 1.0 constant_dynamic-update-slice_fusion
  14.7 0.7 slice_bitcast_fusion.1
  15.5 0.7 pad_maximum_fusion.8
  16.3 1.8 %scatter_fusion.1 = f32[4,16,3,128]{3,2,1,0:T(4,128)S(1)} fusion(f32[4,16,3,128]{3,2,1,0:T(4,128)S(1)} %broadcast_in_dim.67, s32[32]{0:T(128)S(1)} %fusion.22, f32[32,3,128]{2,1,0:T(4,128)S(1)} %copy.34), kind=kCustom, calls=%fused_computation.1 | custom fusion | bytes 147712 | tf_op jit(solution)/shard_map/scatter | solution.py:96
  18.1 0.6 copy.35
  18.8 0.7 broadcast_compare_fusion
  19.5 0.1 copy.30
  19.6 0.1 broadcast_in_dim.63
  19.8 0.1 copy.38
  19.9 0.1 broadcast_in_dim.70
  20.1 0.1 copy.39
  20.2 0.1 broadcast_in_dim.72
  20.4 0.1 copy.40
  20.5 0.1 broadcast_in_dim.74
  20.7 5.1 %all-to-all-start.1 = ((f32[4,16,3,128]{3,1,2,0:T(8,128)}), f32[4,16,3,128]{3,1,2,0:T(8,128)S(1)}, u32[]{:S(2)}, u32[]{:S(2)}) async-start(f32[4,16,3,128]{3,1,2,0:T(8,128)} %copy.35), calls=%async_computation.1 | async-start | bytes 196608 | tf_op jit(solution)/shard_map/all_to_all | solution.py:103
  25.8 0.1 reshape.314
  25.9 0.8 scatter_custom_fusion.3
  26.7 0.1 eq.234
  26.8 0.1 broadcast_in_dim.69
  27.0 0.1 eq.241
  27.2 1.3 %collective-permute-start.1 = (f32[2,65,1]{2,1,0:T(8,128)S(1)}, f32[2,65,1]{2,1,0:T(8,128)S(1)}, u32[]{:S(2)}, u32[]{:S(2)}) collective-permute-start(f32[2,65,1]{2,1,0:T(8,128)S(1)} %slice.210), channel_id=1, source_target_pairs={{1,0},{2,1},{3,2},{5,4},{6,5},{7,6},{9,8},{10,9},{11,10},{13,12},{... | collective-permute-start | bytes 1568 | tf_op jit(solution)/shard_map/ppermute | solution.py:13
  28.5 0.1 broadcast_in_dim.71
  28.7 0.1 eq.248
  28.8 0.1 broadcast_in_dim.73
  29.0 0.1 eq.255
  29.1 0.1 broadcast_in_dim.75
  29.3 4.8 %collective-permute-done.1 = f32[2,65,1]{2,1,0:T(8,128)S(1)} collective-permute-done((f32[2,65,1]{2,1,0:T(8,128)S(1)}, f32[2,65,1]{2,1,0:T(8,128)S(1)}, u32[]{:S(2)}, u32[]{:S(2)}) %collective-permute-start.1) | collective-permute-done | bytes 552 | tf_op jit(solution)/shard_map/ppermute | solution.py:13
  34.2 0.1 copy.37
  34.4 2.4 %scatter_fusion.2 = f32[3,256,128]{2,0,1:T(4,128)S(1)} fusion(f32[3,256,128]{2,0,1:T(4,128)S(1)} %broadcast_in_dim.64, s32[64]{0:T(128)S(1)} %fusion.18, f32[64,3,128]{2,1,0:T(4,128)S(1)} %copy.37), kind=kCustom, calls=%fused_computation.2 | custom fusion | bytes 295168 | tf_op jit(solution)/shard_map/scatter | solution.py:112
  36.8 1.1 slice_reduce_fusion.1
  38.2 0.1 bitcast_dynamic-update-slice_fusion.6
  38.3 0.1 bitcast_dynamic-update-slice_fusion.4
  38.5 0.1 bitcast_dynamic-update-slice_fusion.2
  38.7 0.1 bitcast_dynamic-update-slice_fusion
  38.8 1.9 %collective-permute-start.2 = (f32[12,2,512]{2,1,0:T(2,128)S(1)}, f32[12,2,512]{2,1,0:T(2,128)S(1)}, u32[]{:S(2)}, u32[]{:S(2)}) collective-permute-start(f32[12,2,512]{2,1,0:T(2,128)S(1)} %get-tuple-element.18), channel_id=1, source_target_pairs={{0,4},{4,8},{8,12},{12,16},{16,20},{20,24},{24,28},{1,5},{5,9},{9,... | collective-permute-start | bytes 147464 | tf_op jit(solution)/shard_map/ppermute | solution.py:23
  40.7 1.3 %collective-permute-start.3 = (f32[12,2,512]{2,1,0:T(2,128)S(1)}, f32[12,2,512]{2,1,0:T(2,128)S(1)}, u32[]{:S(2)}, u32[]{:S(2)}) collective-permute-start(f32[12,2,512]{2,1,0:T(2,128)S(1)} %get-tuple-element.19), channel_id=1, source_target_pairs={{4,0},{8,4},{12,8},{16,12},{20,16},{24,20},{28,24},{5,1},{9,5},{13... | collective-permute-start | bytes 147464 | tf_op jit(solution)/shard_map/ppermute | solution.py:24
  42.0 0.1 multiply_bitcast_fusion.3
  42.2 2.8 %collective-permute-done.3 = f32[12,2,512]{2,1,0:T(2,128)S(1)} collective-permute-done((f32[12,2,512]{2,1,0:T(2,128)S(1)}, f32[12,2,512]{2,1,0:T(2,128)S(1)}, u32[]{:S(2)}, u32[]{:S(2)}) %collective-permute-start.3) | collective-permute-done | bytes 49184 | tf_op jit(solution)/shard_map/ppermute | solution.py:24
  45.0 0.2 pad_maximum_fusion.6
  45.2 4.1 %collective-permute-start.4 = (f32[12,68,2]{2,1,0:T(8,128)S(1)}, f32[12,68,2]{2,1,0:T(8,128)S(1)}, u32[]{:S(2)}, u32[]{:S(2)}) collective-permute-start(f32[12,68,2]{2,1,0:T(8,128)S(1)} %get-tuple-element.16), channel_id=1, source_target_pairs={{0,1},{1,2},{2,3},{4,5},{5,6},{6,7},{8,9},{9,10},{10,11},{12,13},{... | collective-permute-start | bytes 19592 | tf_op jit(solution)/shard_map/ppermute | solution.py:23
  49.3 1.5 %collective-permute-start.5 = (f32[12,68,2]{2,1,0:T(8,128)S(1)}, f32[12,68,2]{2,1,0:T(8,128)S(1)}, u32[]{:S(2)}, u32[]{:S(2)}) collective-permute-start(f32[12,68,2]{2,1,0:T(8,128)S(1)} %get-tuple-element.17), channel_id=1, source_target_pairs={{1,0},{2,1},{3,2},{5,4},{6,5},{7,6},{9,8},{10,9},{11,10},{13,12},{... | collective-permute-start | bytes 19592 | tf_op jit(solution)/shard_map/ppermute | solution.py:24
  50.8 7.1 %collective-permute-done.4 = f32[12,68,2]{2,1,0:T(8,128)S(1)} collective-permute-done((f32[12,68,2]{2,1,0:T(8,128)S(1)}, f32[12,68,2]{2,1,0:T(8,128)S(1)}, u32[]{:S(2)}, u32[]{:S(2)}) %collective-permute-start.4) | collective-permute-done | bytes 6560 | tf_op jit(solution)/shard_map/ppermute | solution.py:23
  57.9 4.7 %collective-permute-done.5 = f32[12,68,2]{2,1,0:T(8,128)S(1)} collective-permute-done((f32[12,68,2]{2,1,0:T(8,128)S(1)}, f32[12,68,2]{2,1,0:T(8,128)S(1)}, u32[]{:S(2)}, u32[]{:S(2)}) %collective-permute-start.5) | collective-permute-done | bytes 6560 | tf_op jit(solution)/shard_map/ppermute | solution.py:24
  62.6 1.0 pad_maximum_fusion
  63.6 0.4 slice_add_fusion
  64.0 1.5 %fusion.2 = (f32[12,68,514]{2,1,0:T(8,128)S(1)}, f32[12,68,514]{2,1,0:T(8,128)S(1)}, f32[12,68,514]{2,1,0:T(8,128)S(1)}) fusion(f32[12,68,516]{2,1,0:T(8,128)S(1)} %pad_maximum_fusion, f32[12,68,2]{2,1,0:T(8,128)S(1)} %collective-permute-done.5, f32[12,2,512]{2,1,0:T(2,128)S(1)} %collective-permute-done.3, ...), kind=kLoop, calls=%fused_computation.11 | loop fusion | flops 3355392 | bytes 8395008 | tf_op jit(solution)/shard_map/add | solution.py:30
  65.6 0.3 fusion.1
  65.9 0.6 fusion
  66.5 1.7 %multiply_subtract_fusion = f32[12,64,513]{2,1,0:T(8,128)S(1)} fusion(f32[12,66,514]{2,1,0:T(8,128)S(1)} %fusion, f32[12,68,514]{2,1,0:T(8,128)S(1)} %get-tuple-element.14, f32[12,68,514]{2,1,0:T(8,128)S(1)} %get-tuple-element.15, f32[64,513]{1,0:T(8,128)S(1)} %multiply_bitcast_fusion, f32[64,513]{1,0:T(8,128)S(1)} %get-tuple-element.11), kind=kLoop, calls=%fused_computation.19 | loop fusion | flops 3545856 | bytes 8142336 | tf_op jit(solution)/shard_map/sub | solution.py:38
  68.2 1.1 %multiply_subtract_fusion.1 = f32[12,65,512]{2,1,0:T(8,128)S(1)} fusion(f32[12,66,514]{2,1,0:T(8,128)S(1)} %fusion.1, f32[12,64,512]{2,1,0:T(8,128)S(1)} %bitcast_dynamic-update-slice_fusion, f32[12,2,512]{2,1,0:T(2,128)S(1)} %collective-permute-done.2, f32[12,2,512]{2,1,0:T(2,128)S(1)} %collective-permute-done.3, f32[65,512]{1,0:T(8,128)S(1)} %multiply_bitcast_fusion.2, ...), kind=kLoop, calls=%fused_computation.26 | loop fusion | flops 4392960 | bytes 6729728 | tf_op jit(solution)/shard_map/sub | solution.py:38
  69.3 0.8 slice_subtract_fusion.2
  70.1 0.2 slice_reduce_fusion
  70.3 41.8 %psum.7 = f32[2,4]{0,1:T(4,128)S(1)} all-reduce(f32[2,4]{0,1:T(4,128)S(1)} %bitcast.132), channel_id=1, replica_groups=mesh['gx'=8,'gy'=4] {'gx','gy'}, use_global_device_ids=true, to_apply=%region_7.8 | all-reduce | flops 8 | bytes 64 | tf_op jit(solution)/shard_map/psum | solution.py:134
  112.1 0.6 copy.41
  (49 shorter events, 1.2 us)
Async XLA Ops:
  5.4 15.3 %all-to-all-start = ((f32[4,16,2]{1,2,0:T(2,128)}), f32[4,16,2]{1,2,0:T(2,128)S(1)}, u32[]{:S(2)}, u32[]{:S(2)}) async-start(f32[4,16,2]{1,2,0:T(2,128)} %copy.32), calls=%async_computation | async-start | bytes 8192 | tf_op jit(solution)/shard_map/all_to_all | solution.py:104
  12.5 14.6 %collective-permute-start = (f32[2,1,512]{2,1,0:T(1,128)S(1)}, f32[2,1,512]{2,1,0:T(1,128)S(1)}, u32[]{:S(2)}, u32[]{:S(2)}) collective-permute-start(f32[2,1,512]{2,1,0:T(1,128)S(1)} %slice.171), channel_id=1, source_target_pairs={{4,0},{8,4},{12,8},{16,12},{20,16},{24,20},{28,24},{5,1},{9,5},{13... | collective-permute-start | bytes 12296 | tf_op jit(solution)/shard_map/ppermute | solution.py:13
  20.7 13.5 %all-to-all-start.1 = ((f32[4,16,3,128]{3,1,2,0:T(8,128)}), f32[4,16,3,128]{3,1,2,0:T(8,128)S(1)}, u32[]{:S(2)}, u32[]{:S(2)}) async-start(f32[4,16,3,128]{3,1,2,0:T(8,128)} %copy.35), calls=%async_computation.1 | async-start | bytes 196608 | tf_op jit(solution)/shard_map/all_to_all | solution.py:103
  27.2 6.9 %collective-permute-start.1 = (f32[2,65,1]{2,1,0:T(8,128)S(1)}, f32[2,65,1]{2,1,0:T(8,128)S(1)}, u32[]{:S(2)}, u32[]{:S(2)}) collective-permute-start(f32[2,65,1]{2,1,0:T(8,128)S(1)} %slice.210), channel_id=1, source_target_pairs={{1,0},{2,1},{3,2},{5,4},{6,5},{7,6},{9,8},{10,9},{11,10},{13,12},{... | collective-permute-start | bytes 1568 | tf_op jit(solution)/shard_map/ppermute | solution.py:13
  34.1 3.9 %copy-start = (f32[64,512]{1,0:T(8,128)S(1)}, f32[64,512]{1,0:T(8,128)}, u32[]{:S(2)}) copy-start(f32[64,512]{1,0:T(8,128)} %param.7) | copy-start | bytes 393220
  34.2 3.9 %copy-start.2 = (f32[64,512]{1,0:T(8,128)S(1)}, f32[64,512]{1,0:T(8,128)}, u32[]{:S(2)}) copy-start(f32[64,512]{1,0:T(8,128)} %param.8) | copy-start | bytes 393220
  38.8 3.3 %collective-permute-start.2 = (f32[12,2,512]{2,1,0:T(2,128)S(1)}, f32[12,2,512]{2,1,0:T(2,128)S(1)}, u32[]{:S(2)}, u32[]{:S(2)}) collective-permute-start(f32[12,2,512]{2,1,0:T(2,128)S(1)} %get-tuple-element.18), channel_id=1, source_target_pairs={{0,4},{4,8},{8,12},{12,16},{16,20},{20,24},{24,28},{1,5},{5,9},{9,... | collective-permute-start | bytes 147464 | tf_op jit(solution)/shard_map/ppermute | solution.py:23
  40.7 4.2 %collective-permute-start.3 = (f32[12,2,512]{2,1,0:T(2,128)S(1)}, f32[12,2,512]{2,1,0:T(2,128)S(1)}, u32[]{:S(2)}, u32[]{:S(2)}) collective-permute-start(f32[12,2,512]{2,1,0:T(2,128)S(1)} %get-tuple-element.19), channel_id=1, source_target_pairs={{4,0},{8,4},{12,8},{16,12},{20,16},{24,20},{28,24},{5,1},{9,5},{13... | collective-permute-start | bytes 147464 | tf_op jit(solution)/shard_map/ppermute | solution.py:24
  45.2 12.7 %collective-permute-start.4 = (f32[12,68,2]{2,1,0:T(8,128)S(1)}, f32[12,68,2]{2,1,0:T(8,128)S(1)}, u32[]{:S(2)}, u32[]{:S(2)}) collective-permute-start(f32[12,68,2]{2,1,0:T(8,128)S(1)} %get-tuple-element.16), channel_id=1, source_target_pairs={{0,1},{1,2},{2,3},{4,5},{5,6},{6,7},{8,9},{9,10},{10,11},{12,13},{... | collective-permute-start | bytes 19592 | tf_op jit(solution)/shard_map/ppermute | solution.py:23
  49.3 13.3 %collective-permute-start.5 = (f32[12,68,2]{2,1,0:T(8,128)S(1)}, f32[12,68,2]{2,1,0:T(8,128)S(1)}, u32[]{:S(2)}, u32[]{:S(2)}) collective-permute-start(f32[12,68,2]{2,1,0:T(8,128)S(1)} %get-tuple-element.17), channel_id=1, source_target_pairs={{1,0},{2,1},{3,2},{5,4},{6,5},{7,6},{9,8},{10,9},{11,10},{13,12},{... | collective-permute-start | bytes 19592 | tf_op jit(solution)/shard_map/ppermute | solution.py:24
  70.1 42.6 %copy-start.1 = (f32[12,64,512]{2,1,0:T(8,128)}, f32[12,64,512]{2,1,0:T(8,128)S(1)}, u32[]{:S(2)}) copy-start(f32[12,64,512]{2,1,0:T(8,128)S(1)} %slice_subtract_fusion.2) | copy-start | bytes 4718596
where the time goes:
time: 113 us
  blocking collectives  41.8 us (37%)
  starting transfers between devices  22.7 us (20%)
  waiting for transfers between devices  19.5 us (17%)
  local copies, waits for them, and re-layouts  16.4 us (15%)
  other arithmetic  11.1 us (10%)
  between operations  1.19 us (1%)
    psum x1, blocking collectives, local(): totals = lax.psum(jnp.sum(remapped[:, 1:], axis=(2, 3)).T, ('gx', 'gy'))  41.8 us
    ppermute x2, waiting for transfers between devices, padded_2(): after = lax.ppermute(first, axis, down)  7.51 us
    ppermute x2, waiting for transfers between devices, padded_2(): before = lax.ppermute(last, axis, up)  7.13 us
    all_to_all x1, starting transfers between devices, local(): lax.all_to_all(outgoing_labels, 'gy', split_axis=0, concat_axis=0, tiled=...  6.32 us
    ppermute x2, starting transfers between devices, padded_2(): before = lax.ppermute(last, axis, up)  5.97 us
    all_to_all x1, starting transfers between devices, local(): lax.all_to_all(outgoing, 'gy', split_axis=0, concat_axis=0, tiled=True)  5.1 us
    ppermute x2, waiting for transfers between devices, passed_along(): lax.ppermute(value, axis, [(source, source + steps) for source in range(f...  4.85 us
    scatter x2, local copies, waits for them, and re-layouts, local(): jnp.full((gy_count, cap_slots, 2), -1.0, jnp.float32)  2.84 us
  transfers between devices with their start and end apart: 8, of which 4 were waited for; matrix products, arithmetic and copies ran while one was open for 9% of the time, Pallas kernels for 0%

commit v1 on v0

v1 whole, which is shorter than its diff:
```python
import functools
import jax
import jax.numpy as jnp
from jax import lax
from jax.experimental import pallas as pl
from jax.experimental.pallas import tpu as pltpu
from jax.sharding import PartitionSpec as P

M = 4
F = 3 * M
TILE = 128
MESH = pl.DeviceIdType.MESH
f32 = jnp.float32
bf16 = jnp.bfloat16
NT = (((1,), (1,)), ((), ()))


def iota(shape, dim):
    return lax.broadcasted_iota(jnp.int32, shape, dim)


def split3(x):
    hi = x.astype(bf16)
    rest = x - hi.astype(f32)
    mid = rest.astype(bf16)
    low = (rest - mid.astype(f32)).astype(bf16)
    return hi, mid, low


def pick(onehot, data):
    parts = split3(data)
    o = onehot.astype(bf16)
    total = jnp.dot(o, parts[2], preferred_element_type=f32)
    total = total + jnp.dot(o, parts[1], preferred_element_type=f32)
    return total + jnp.dot(o, parts[0], preferred_element_type=f32)


def kernel(
    ngx, ngy, cap,
    density, energy, disp, tile_mat, frac, state, route,
    out, totals,
    send1, got1, drow, drow_in, dcol, dcol_in, de, ax, bx, ay, by,
    q, pk, xs, cols_in, rows_in, part, tot_y, tot_x, tot_sum,
    s1, r1, s2, r2, s3, r3, sy, ry, sx, rx,
):
    gx, gy = lax.axis_index("gx"), lax.axis_index("gy")
    rows, width = density.shape
    ext = width + TILE
    full = rows + 16
    per_row = width // TILE
    slots = frac.shape[0]
    up, down = gx > 0, gx < ngx - 1
    left, right = gy > 0, gy < ngy - 1

    def exists(dx, dy):
        ok = True
        if dx:
            ok = up if dx < 0 else down
        if dy:
            side = left if dy < 0 else right
            ok = side if ok is True else jnp.logical_and(ok, side)
        return ok

    barrier = pltpu.get_barrier_semaphore()
    diagonals = [(-1, -1), (-1, 1), (1, -1), (1, 1)]
    for k in range(1, ngy):
        pl.semaphore_signal(barrier, inc=1, device_id=(gx, lax.rem(gy + k, ngy)), device_id_type=MESH)
    for k in range(1, ngx):
        pl.semaphore_signal(barrier, inc=1, device_id=(lax.rem(gx + k, ngx), gy), device_id_type=MESH)
    for dx, dy in diagonals:
        @pl.when(exists(dx, dy))
        def _(dx=dx, dy=dy):
            pl.semaphore_signal(barrier, inc=1, device_id=(gx + dx, gy + dy), device_id_type=MESH)

    count = ngy * cap
    target = route[0:1, :]
    row = iota((count, slots), 0)
    wanted = lax.rem(gy + row // cap, ngy)
    member = (jnp.broadcast_to(target, (count, slots)) == wanted).astype(f32)
    before = (iota((slots, slots), 0) < iota((slots, slots), 1)).astype(bf16)
    rank = jnp.dot(member.astype(bf16), before, preferred_element_type=f32)
    chosen = jnp.where(rank == (row % cap).astype(f32), member, 0.0)
    payload = jnp.concatenate([frac[...], state[0], state[1]], axis=1)
    packed = pick(chosen, payload)
    named = jnp.concatenate(
        [(route[1:3, :] + 1).astype(f32), jnp.zeros((6, slots), f32)], axis=0
    )
    labels = lax.dot_general(
        named, chosen, NT, precision=lax.Precision.HIGHEST, preferred_element_type=f32
    )
    label_lane = iota((8, count), 1) // cap
    wide = send1.shape[2]
    for k in range(ngy):
        dst = got1 if k == 0 else send1
        dst[k, 0:cap, 0 : 3 * TILE] = packed[k * cap : (k + 1) * cap]
        dst[k, cap : cap + 8, 0:count] = jnp.where(label_lane == k, labels, 0.0)

    drow[...] = jnp.concatenate([disp[0, 0:8][0:1], disp[1, 0:8][0:1], jnp.zeros((6, width), f32)], axis=0)
    lane_r = iota((rows, TILE), 1)
    dcol[...] = jnp.where(lane_r == 0, disp[0, :, 0:TILE], pltpu.roll(disp[1, :, 0:TILE], 1, 1))

    diag_count = sum(exists(dx, dy).astype(jnp.int32) for dx, dy in diagonals)
    pl.semaphore_wait(barrier, ngy - 1 + ngx - 1 + diag_count)

    def remote(src, dst, s, r, to):
        return pltpu.make_async_remote_copy(
            src_ref=src, dst_ref=dst, send_sem=s, recv_sem=r, device_id=to, device_id_type=MESH
        )

    tile_copies = [
        remote(send1.at[k], got1.at[k], s1.at[k], r1.at[k], (gx, lax.rem(gy + k, ngy)))
        for k in range(1, ngy)
    ]
    for c in tile_copies:
        c.start()
    disp_moves = [
        ((-1, 0), remote(drow, drow_in, s3.at[0], r3.at[0], (gx - 1, gy))),
        ((0, -1), remote(dcol, dcol_in.at[0:rows], s3.at[1], r3.at[1], (gx, gy - 1))),
        ((-1, -1), remote(dcol.at[0:8], dcol_in.at[rows : rows + 8], s3.at[2], r3.at[2], (gx - 1, gy - 1))),
    ]
    for (dx, dy), c in disp_moves:
        @pl.when(exists(dx, dy))
        def _(c=c):
            c.start()

    @pl.when(jnp.logical_not(down))
    def _():
        drow_in[...] = jnp.zeros(drow_in.shape, f32)

    @pl.when(jnp.logical_not(right))
    def _():
        dcol_in[0:rows] = jnp.zeros((rows, TILE), f32)

    @pl.when(jnp.logical_not(exists(1, 1)))
    def _():
        dcol_in[rows : rows + 8] = jnp.zeros((8, TILE), f32)

    def row_span(dx):
        return {1: slice(0, 8), 0: slice(8, 8 + rows), -1: slice(8 + rows, full)}[dx]

    def col_span(dx):
        return {1: slice(rows - 8, rows), 0: slice(0, rows), -1: slice(0, 8)}[dx]

    def halo_copy(n, dx, dy):
        to = (gx + dx, gy + dy)
        if dy == 0:
            src, dst = xs.at[1 if dx > 0 else 0], rows_in.at[0 if dx > 0 else 1]
        else:
            src = pk.at[col_span(dx)]
            dst = cols_in.at[0 if dy > 0 else 1, row_span(dx)]
        return remote(src, dst, s2.at[n], r2.at[n], to)

    directions = [(0, 1), (0, -1)] + diagonals + [(1, 0), (-1, 0)]
    halo = [(dx, dy, halo_copy(n, dx, dy)) for n, (dx, dy) in enumerate(directions)]
    for dx, dy, _c in halo:
        @pl.when(jnp.logical_not(exists(-dx, -dy)))
        def _(dx=dx, dy=dy):
            if dy == 0:
                rows_in[0 if dx > 0 else 1] = jnp.zeros(rows_in.shape[1:], f32)
            else:
                span = row_span(dx)
                cols_in[0 if dy > 0 else 1, span] = jnp.zeros((span.stop - span.start, TILE), f32)

    zero8 = jnp.zeros((8, ext), f32)
    for f in range(F):
        q[f, 0:8] = zero8
        q[f, full - 8 : full] = zero8

    for c in tile_copies:
        c.wait_recv()
    label = got1[0, cap : cap + 8, 0:count]
    for k in range(1, ngy):
        label = label + got1[k, cap : cap + 8, 0:count]
    tiles = per_row * rows
    place = iota((tiles, count), 0)
    place = (place % rows) * per_row + place // rows + 1
    hit = (jnp.broadcast_to(label[0:1, :].astype(jnp.int32), (tiles, count)) == place).astype(f32)
    arrived = jnp.concatenate([got1[k, 0:cap, 0 : 3 * TILE] for k in range(ngy)], axis=0)
    mixed = pick(hit, arrived)
    second = jnp.dot(
        (hit * label[1:2, :]).astype(bf16), jnp.ones((count, TILE), bf16), preferred_element_type=f32
    )
    edge = []
    for c in [0] + list(range(per_row - 1, 0, -1)):
        at = slice(c * rows, (c + 1) * rows)
        lanes = slice(c * TILE, (c + 1) * TILE)
        fr, d2, e2 = (mixed[at, n * TILE : (n + 1) * TILE] for n in range(3))
        other_m = second[at]
        own_m = jnp.broadcast_to(tile_mat[:, c : c + 1], (rows, TILE))
        d1 = density[:, lanes]
        e1 = energy[:, lanes]
        de1 = d1 * e1
        de2 = d2 * e2
        clear = 1.0 - fr
        for m in range(M):
            own = jnp.where(own_m == m, clear, 0.0)
            oth = jnp.where(other_m == m + 1.0, fr, 0.0)
            for n, value in enumerate((own + oth, own * d1 + oth * d2, own * de1 + oth * de2)):
                q[3 * m + n, 8 : 8 + rows, lanes] = value
    acc = jnp.zeros((rows, TILE), f32)
    for f in range(F):
        both = jnp.where(
            lane_r < TILE // 2, q[f, 8 : 8 + rows, 0:TILE], q[f, 8 : 8 + rows, width - TILE : width]
        )
        acc = jnp.where(lane_r // 4 == f, pltpu.roll(both, 4 * f + 2, 1), acc)
    pk[...] = acc
    for dx, dy, c in halo[:6]:
        @pl.when(exists(dx, dy))
        def _(c=c):
            c.start()
    for f in range(F):
        xs[0, 2 * f : 2 * f + 2] = q[f, 8:16, 0:width][0:2]
        xs[1, 2 * f : 2 * f + 2] = q[f, rows : rows + 8, 0:width][6:8]
    for dx, dy, c in halo[6:]:
        @pl.when(exists(dx, dy))
        def _(c=c):
            c.start()

    for (dx, dy), c in disp_moves:
        @pl.when(exists(-dx, -dy))
        def _(c=c):
            c.wait_recv()
    dc = dcol_in[...]
    for c in range(2):
        de[c, 0:rows, 0:width] = disp[c]
        de[c, rows : rows + 8, 0:width] = jnp.broadcast_to(drow_in[c : c + 1, :], (8, width))
        de[c, :, width:ext] = dc if c == 0 else pltpu.roll(dc, TILE - 1, 1)
    face = iota((rows + 8, ext), 0)
    closed_x = jnp.logical_or(
        jnp.logical_and(face == 0, jnp.logical_not(up)), jnp.logical_and(face == rows, jnp.logical_not(down))
    )
    d0 = de[0]
    speed = jnp.where(closed_x, 0.0, -0.5 * (d0 + pltpu.roll(d0, ext - 1, 1)))
    ax[...] = jnp.maximum(speed, 0.0)
    bx[...] = jnp.minimum(speed, 0.0)
    face = iota((rows, ext), 1)
    closed_y = jnp.logical_or(
        jnp.logical_and(face == 0, jnp.logical_not(left)), jnp.logical_and(face == width, jnp.logical_not(right))
    )
    d1 = de[1]
    speed = jnp.where(closed_y, 0.0, -0.5 * (d1[0:rows] + pltpu.roll(d1, rows + 7, 0)[0:rows]))
    ay[...] = jnp.maximum(speed, 0.0)
    by[...] = jnp.minimum(speed, 0.0)

    for dx, dy, c in halo:
        @pl.when(exists(-dx, -dy))
        def _(c=c):
            c.wait_recv()
    lane_f = iota((full, TILE), 1)
    ring = jnp.where(lane_f % 4 < 2, cols_in[0], cols_in[1])
    for f in range(F):
        q[f, :, width:ext] = pltpu.roll(ring, TILE - 4 * f - 2, 1)
        q[f, 6:8, 0:width] = rows_in[0, 2 * f : 2 * f + 2]
        q[f, 8 + rows : 10 + rows, 0:width] = rows_in[1, 2 * f : 2 * f + 2]

    blocks = full // 8
    sub = iota((8, ext), 0)
    twelfth = 1.0 / 12.0

    def one_field(f, carry):
        qs, sums, diffs, hs, fluxes = {}, {}, {}, {}, {}

        def load(b):
            if b not in qs:
                v = q[f, b * 8 : b * 8 + 8]
                before, after = pltpu.roll(v, 1, 1), pltpu.roll(v, ext - 1, 1)
                qs[b], sums[b], diffs[b] = v, v + before + after, after - before

        def prev(values, b):
            if b == 0:
                return pltpu.roll(values[b], 1, 0)
            return pltpu.roll(jnp.where(sub == 7, values[b - 1], values[b]), 1, 0)

        def follow(values, b):
            if b == blocks - 1:
                return pltpu.roll(values[b], 7, 0)
            return pltpu.roll(jnp.where(sub == 0, values[b + 1], values[b]), 7, 0)

        low, high = {}, {}

        def sides(b):
            if b not in low:
                for n in (b - 1, b, b + 1):
                    if 0 <= n < blocks:
                        load(n)
                h = (follow(sums, b) - prev(sums, b)) * twelfth
                low[b], high[b] = qs[b] + h, qs[b] - h

        def flux(b):
            if b not in fluxes:
                sides(b - 1)
                sides(b)
                at = slice(b * 8 - 8, b * 8)
                fluxes[b] = ax[at] * prev(low, b) + bx[at] * high[b]

        total = jnp.zeros((8, width), f32)
        for b in range(1, blocks - 1):
            flux(b)
            flux(b + 1)
            at = slice(b * 8 - 8, b * 8)
            h = (diffs[b] + prev(diffs, b) + follow(diffs, b)) * twelfth
            fy = ay[at] * pltpu.roll(qs[b] + h, 1, 1) + by[at] * (qs[b] - h)
            value = qs[b] + fluxes[b] - follow(fluxes, b) + fy - pltpu.roll(fy, ext - 1, 1)
            value = value[:, 0:width]
            out[f, at] = value
            total = total + value
        lanes = total[:, 0:TILE]
        for c in range(1, per_row):
            lanes = lanes + total[:, c * TILE : (c + 1) * TILE]
        part[f] = lanes
        return carry

    lax.fori_loop(0, F, one_field, 0)

    mine = jnp.concatenate(
        [jnp.sum(part[3 * m + n], axis=0, keepdims=True) for m in range(M) for n in (1, 2)], axis=0
    )
    tot_y[gy] = mine
    copies = [
        remote(tot_y.at[gy], tot_y.at[gy], sy.at[k], ry.at[k], (gx, lax.rem(gy + k, ngy)))
        for k in range(1, ngy)
    ]
    for c in copies:
        c.start()
    incoming = [
        remote(tot_y.at[lax.rem(gy + ngy - k, ngy)], tot_y.at[lax.rem(gy + ngy - k, ngy)], sy.at[k], ry.at[k],
               (gx, lax.rem(gy + k, ngy)))
        for k in range(1, ngy)
    ]
    for c in incoming:
        c.wait_recv()
    mine = tot_y[0]
    for k in range(1, ngy):
        mine = mine + tot_y[k]
    tot_x[gx] = mine
    copies_x = [
        remote(tot_x.at[gx], tot_x.at[gx], sx.at[k], rx.at[k], (lax.rem(gx + k, ngx), gy))
        for k in range(1, ngx)
    ]
    for c in copies_x:
        c.start()
    incoming = [
        remote(tot_x.at[lax.rem(gx + ngx - k, ngx)], tot_x.at[lax.rem(gx + ngx - k, ngx)], sx.at[k], rx.at[k],
               (lax.rem(gx + k, ngx), gy))
        for k in range(1, ngx)
    ]
    for c in incoming:
        c.wait_recv()
    mine = tot_x[0]
    for k in range(1, ngx):
        mine = mine + tot_x[k]
    whole = jnp.broadcast_to(jnp.sum(mine, axis=1, keepdims=True), (2 * M, TILE))
    r8, l8 = iota((2 * M, TILE), 0), iota((2 * M, TILE), 1)
    for n in range(2):
        line = jnp.sum(jnp.where(r8 == 2 * l8 + n, whole, 0.0), axis=0, keepdims=True)
        totals[n : n + 1, :] = line[:, 0:M]

    for c in tile_copies + copies + copies_x:
        c.wait_send()
    for (dx, dy), c in disp_moves:
        @pl.when(exists(dx, dy))
        def _(c=c):
            c.wait_send()
    for dx, dy, c in halo:
        @pl.when(exists(dx, dy))
        def _(c=c):
            c.wait_send()


def local(ngx, ngy, density, energy, displacement, tile_mat, store_frac, store_state, store_route):
    rows, width = density.shape
    cap = rows * (width // TILE) // 16
    ext, full = width + TILE, rows + 16
    wide = -(-max(3 * TILE, ngy * cap) // TILE) * TILE
    vmem, dma = pltpu.VMEM, pltpu.SemaphoreType.DMA
    spec = pl.BlockSpec(memory_space=pltpu.VMEM)
    scratch = [
        vmem((ngy, cap + 8, wide), f32),
        vmem((ngy, cap + 8, wide), f32),
        vmem((8, width), f32),
        vmem((8, width), f32),
        vmem((rows, TILE), f32),
        vmem((rows + 8, TILE), f32),
        vmem((2, rows + 8, ext), f32),
        vmem((rows + 8, ext), f32),
        vmem((rows + 8, ext), f32),
        vmem((rows, ext), f32),
        vmem((rows, ext), f32),
        vmem((F, full, ext), f32),
        vmem((rows, TILE), f32),
        vmem((2, 2 * F, width), f32),
        vmem((2, full, TILE), f32),
        vmem((2, 2 * F, width), f32),
        vmem((F, 8, TILE), f32),
        vmem((ngy, 2 * M, TILE), f32),
        vmem((ngx, 2 * M, TILE), f32),
        vmem((8, TILE), f32),
        dma((ngy,)), dma((ngy,)), dma((8,)), dma((8,)), dma((3,)), dma((3,)),
        dma((ngy,)), dma((ngy,)), dma((ngx,)), dma((ngx,)),
    ]
    remapped, totals = pl.pallas_call(
        functools.partial(kernel, ngx, ngy, cap),
        out_shape=(jax.ShapeDtypeStruct((F, rows, width), f32), jax.ShapeDtypeStruct((2, M), f32)),
        in_specs=[spec] * 7,
        out_specs=(spec, spec),
        scratch_shapes=scratch,
        compiler_params=pltpu.CompilerParams(
            collective_id=0, has_side_effects=True, vmem_limit_bytes=40 * 1024 * 1024
        ),
    )(density, energy, displacement, tile_mat, store_frac, store_state, store_route)
    return remapped.reshape(M, 3, rows, width), totals


def solution(mesh):
    placed = (
        P("gx", "gy"),
        P("gx", "gy"),
        P(None, "gx", "gy"),
        P("gx", "gy"),
        P(("gx", "gy"), None),
        P(None, ("gx", "gy"), None),
        P(None, ("gx", "gy")),
    )
    return jax.shard_map(
        functools.partial(local, mesh.shape["gx"], mesh.shape["gy"]),
        mesh=mesh,
        in_specs=placed,
        out_specs=(P(None, None, "gx", "gy"), P()),
        check_vma=False,
    )
```

time: 113 us -> 34.8 us (0.31)
  blocking collectives: 41.8 us -> 0 us
  Pallas kernels: 0 us -> 26.4 us
  starting transfers between devices: 22.7 us -> 0 us
  waiting for transfers between devices: 19.5 us -> 0 us
  other arithmetic: 11.1 us -> 0 us
  local copies, waits for them, and re-layouts: 16.4 us -> 7.39 us
    psum x1 -> x0, blocking collectives: 41.8 us -> none  [local(): totals = lax.psum(jnp.sum(remapped[:, 1:], axis=(2, 3)).T, ('gx', 'gy'))]
    pallas_call x0 -> x1, Pallas kernels: none -> 26.4 us  [local(): pl.pallas_call(functools.partial(kernel, ngx, ngy, cap), out_shape=(jax.S...]
    ppermute x6 -> x0, waiting for transfers between devices: 19.5 us -> none  [the longest x2 7.51 us: padded_2(): after = lax.ppermute(first, axis, down)]
    all_to_all x2 -> x0, starting transfers between devices: 11.4 us -> none  [the longest x1 6.32 us: local(): lax.all_to_all(outgoing_labels, 'gy', split_axis=0, concat_axis=0, tiled=...]
    ppermute x6 -> x0, starting transfers between devices: 11.3 us -> none  [the longest x2 5.97 us: padded_2(): before = lax.ppermute(last, axis, up)]
    scatter x6 -> x0, local copies, waits for them, and re-layouts: 8.53 us -> none  [the longest x2 2.84 us: local(): jnp.full((gy_count, cap_slots, 2), -1.0, jnp.float32)]
    unnamed x8 -> x15, local copies, waits for them, and re-layouts: 1.64 us -> 7.39 us
    sub x3 -> x0, other arithmetic: 3.58 us -> none  [the longest x2 2.82 us: upwind(): face_speed * 0.5 * (lower_side + upper_side)]
  transfers between devices with their start and end apart: 8 -> 0, of which waited for: 4 -> 0; matrix products, arithmetic and copies ran while one was open for 9% -> 0% of each run, Pallas kernels for 0% -> 0%
where the time goes in v1:
time: 34.8 us; the launch traced here: 34.5 us
  Pallas kernels  26.4 us (76%)
  local copies, waits for them, and re-layouts  7.39 us (21%)
  between operations  0.64 us (2%)
    pallas_call x1, Pallas kernels, local(): pl.pallas_call(functools.partial(kernel, ngx, ngy, cap), out_shape=(jax.S...  26.4 us
    unnamed x15, local copies, waits for them, and re-layouts  7.39 us

profile of v1, /device:TPU:0, one launch (start us, length us, event | category | flops | bytes accessed | tf_op | source)
XLA Modules:
  0.0 34.5 jit_solution(818458953110374561)
XLA Ops:
  0.6 0.8 %copy.9.tile_mat = s32[64,4]{1,0:T(8,128)S(1)} copy(s32[64,4]{0,1:T(4,128)} %param.10) | data formatting | bytes 2048 | tf_op args[3]
  1.4 0.0 copy-start
  1.4 0.9 %copy-done = f32[2,64,512]{2,1,0:T(8,128)S(1)} copy-done((f32[2,64,512]{2,1,0:T(8,128)S(1)}, f32[2,64,512]{2,1,0:T(8,128)}, u32[]{:S(2)}) %copy-start) | copy-done | bytes 262168
  2.4 0.0 copy-start.1
  2.4 0.9 %copy-done.1 = f32[64,512]{1,0:T(8,128)S(1)} copy-done((f32[64,512]{1,0:T(8,128)S(1)}, f32[64,512]{1,0:T(8,128)}, u32[]{:S(2)}) %copy-start.1) | copy-done | bytes 131096
  3.3 0.0 copy-start.2
  3.3 0.9 %copy-done.2 = f32[64,512]{1,0:T(8,128)S(1)} copy-done((f32[64,512]{1,0:T(8,128)S(1)}, f32[64,512]{1,0:T(8,128)}, u32[]{:S(2)}) %copy-start.2) | copy-done | bytes 131096
  4.2 0.0 copy-start.3
  4.2 0.8 %copy-done.3 = f32[2,32,128]{2,1,0:T(8,128)S(1)} copy-done((f32[2,32,128]{2,1,0:T(8,128)S(1)}, f32[2,32,128]{2,1,0:T(8,128)}, u32[]{:S(2)}) %copy-start.3) | copy-done | bytes 32792
  4.9 0.0 copy-start.4
  4.9 0.7 %copy-done.4 = f32[32,128]{1,0:T(8,128)S(1)} copy-done((f32[32,128]{1,0:T(8,128)S(1)}, f32[32,128]{1,0:T(8,128)}, u32[]{:S(2)}) %copy-start.4) | copy-done | bytes 16408
  5.6 0.0 copy-start.5
  5.6 0.7 %copy-done.5 = s32[3,32]{1,0:T(4,128)S(1)} copy-done((s32[3,32]{1,0:T(4,128)S(1)}, s32[3,32]{1,0:T(4,128)}, u32[]{:S(2)}) %copy-start.5) | copy-done | bytes 408
  6.3 26.4 %shard_map.86 = (f32[12,64,512]{2,1,0:T(8,128)S(1)}, f32[2,4]{1,0:T(2,128)S(1)}) custom-call(f32[64,512]{1,0:T(8,128)S(1)} %copy-done.1, f32[64,512]{1,0:T(8,128)S(1)} %copy-done.2, f32[2,64,512]{2,1,0:T(8,128)S(1)} %copy-done, s32[64,4]{1,0:T(8,128)S(1)} %copy.9.tile_mat, f32[32,128]{1,0:T(8,128)S(1)} %copy-done.4, f32[2,32,128]{2,1,0:T(8,128)S(1)} %copy-done.3, ...), custom_call_target="tpu_custom_call" | custom-call | tf_op jit(solution)/shard_map/pallas_call | solution.py:401
  32.8 1.1 %copy.12 = f32[4,3,64,512]{3,2,1,0:T(8,128)} copy(f32[4,3,64,512]{3,2,1,0:T(8,128)S(1)} %bitcast.1) | data formatting | bytes 3145728
  33.9 0.6 %copy.13 = f32[2,4]{1,0:T(2,128)} copy(f32[2,4]{1,0:T(2,128)S(1)} %get-tuple-element.9) | data formatting | bytes 64
Async XLA Ops:
  1.4 0.9 %copy-start = (f32[2,64,512]{2,1,0:T(8,128)S(1)}, f32[2,64,512]{2,1,0:T(8,128)}, u32[]{:S(2)}) copy-start(f32[2,64,512]{2,1,0:T(8,128)} %disp.1) | copy-start | bytes 786436
  2.4 0.9 %copy-start.1 = (f32[64,512]{1,0:T(8,128)S(1)}, f32[64,512]{1,0:T(8,128)}, u32[]{:S(2)}) copy-start(f32[64,512]{1,0:T(8,128)} %density.1) | copy-start | bytes 393220
  3.3 0.9 %copy-start.2 = (f32[64,512]{1,0:T(8,128)S(1)}, f32[64,512]{1,0:T(8,128)}, u32[]{:S(2)}) copy-start(f32[64,512]{1,0:T(8,128)} %energy.1) | copy-start | bytes 393220
  4.2 0.8 %copy-start.3 = (f32[2,32,128]{2,1,0:T(8,128)S(1)}, f32[2,32,128]{2,1,0:T(8,128)}, u32[]{:S(2)}) copy-start(f32[2,32,128]{2,1,0:T(8,128)} %state.1) | copy-start | bytes 98308
  4.9 0.7 %copy-start.4 = (f32[32,128]{1,0:T(8,128)S(1)}, f32[32,128]{1,0:T(8,128)}, u32[]{:S(2)}) copy-start(f32[32,128]{1,0:T(8,128)} %frac.1) | copy-start | bytes 49156
  5.6 0.7 %copy-start.5 = (s32[3,32]{1,0:T(4,128)S(1)}, s32[3,32]{1,0:T(4,128)}, u32[]{:S(2)}) copy-start(s32[3,32]{1,0:T(4,128)} %route.1) | copy-start | bytes 1156

commit v2 on v1

--- a/solution.py
+++ b/solution.py
@@ -37,9 +37,10 @@
 
 def kernel(
     ngx, ngy, cap,
-    density, energy, disp, tile_mat, frac, state, route,
-    out, totals,
-    send1, got1, drow, drow_in, dcol, dcol_in, de, ax, bx, ay, by,
+    density_h, energy_h, disp_h, mat_h, frac_h, state_h, route_h,
+    out_h, totals,
+    out, so, density, energy, disp, mat, frac, state, route, s0,
+    primary, send1, got1, drow, drow_in, dcol, dcol_in, de, ax, bx, ay, by,
     q, pk, xs, cols_in, rows_in, part, tot_y, tot_x, tot_sum,
     s1, r1, s2, r2, s3, r3, sy, ry, sx, rx,
 ):
@@ -61,6 +62,18 @@
             ok = side if ok is True else jnp.logical_and(ok, side)
         return ok
 
+    loads = [
+        pltpu.make_async_copy(src, dst, s0.at[n])
+        for n, (src, dst) in enumerate(
+            (
+                (route_h, route), (frac_h, frac), (state_h, state), (disp_h, disp),
+                (mat_h, mat), (density_h, density), (energy_h, energy),
+            )
+        )
+    ]
+    for c in loads:
+        c.start()
+
     barrier = pltpu.get_barrier_semaphore()
     diagonals = [(-1, -1), (-1, 1), (1, -1), (1, 1)]
     for k in range(1, ngy):
@@ -73,6 +86,7 @@
             pl.semaphore_signal(barrier, inc=1, device_id=(gx + dx, gy + dy), device_id_type=MESH)
 
     count = ngy * cap
+    loads[0].wait()
     target = route[0:1, :]
     row = iota((count, slots), 0)
     wanted = lax.rem(gy + row // cap, ngy)
@@ -80,6 +94,8 @@
     before = (iota((slots, slots), 0) < iota((slots, slots), 1)).astype(bf16)
     rank = jnp.dot(member.astype(bf16), before, preferred_element_type=f32)
     chosen = jnp.where(rank == (row % cap).astype(f32), member, 0.0)
+    loads[1].wait()
+    loads[2].wait()
     payload = jnp.concatenate([frac[...], state[0], state[1]], axis=1)
     packed = pick(chosen, payload)
     named = jnp.concatenate(
@@ -95,6 +111,7 @@
         dst[k, 0:cap, 0 : 3 * TILE] = packed[k * cap : (k + 1) * cap]
         dst[k, cap : cap + 8, 0:count] = jnp.where(label_lane == k, labels, 0.0)
 
+    loads[3].wait()
     drow[...] = jnp.concatenate([disp[0, 0:8][0:1], disp[1, 0:8][0:1], jnp.zeros((6, width), f32)], axis=0)
     lane_r = iota((rows, TILE), 1)
     dcol[...] = jnp.where(lane_r == 0, disp[0, :, 0:TILE], pltpu.roll(disp[1, :, 0:TILE], 1, 1))
@@ -165,6 +182,14 @@
     for f in range(F):
         q[f, 0:8] = zero8
         q[f, full - 8 : full] = zero8
+
+    for c in loads[4:]:
+        c.wait()
+    eye = iota((rows, rows), 0) == iota((rows, rows), 1)
+    spread = jnp.concatenate(
+        [jnp.where(eye, mat[c : c + 1, :].astype(f32), 0.0).astype(bf16) for c in range(per_row)], axis=0
+    )
+    primary[...] = jnp.dot(spread, jnp.ones((rows, TILE), bf16), preferred_element_type=f32)
 
     for c in tile_copies:
         c.wait_recv()
@@ -186,14 +211,14 @@
         lanes = slice(c * TILE, (c + 1) * TILE)
         fr, d2, e2 = (mixed[at, n * TILE : (n + 1) * TILE] for n in range(3))
         other_m = second[at]
-        own_m = jnp.broadcast_to(tile_mat[:, c : c + 1], (rows, TILE))
+        own_m = primary[at]
         d1 = density[:, lanes]
         e1 = energy[:, lanes]
         de1 = d1 * e1
         de2 = d2 * e2
         clear = 1.0 - fr
         for m in range(M):
-            own = jnp.where(own_m == m, clear, 0.0)
+            own = jnp.where(own_m == float(m), clear, 0.0)
             oth = jnp.where(other_m == m + 1.0, fr, 0.0)
             for n, value in enumerate((own + oth, own * d1 + oth * d2, own * de1 + oth * de2)):
                 q[3 * m + n, 8 : 8 + rows, lanes] = value
@@ -308,6 +333,7 @@
         for c in range(1, per_row):
             lanes = lanes + total[:, c * TILE : (c + 1) * TILE]
         part[f] = lanes
+        pltpu.make_async_copy(out.at[f], out_h.at[f], so.at[f]).start()
         return carry
 
     lax.fori_loop(0, F, one_field, 0)
@@ -355,6 +381,8 @@
         line = jnp.sum(jnp.where(r8 == 2 * l8 + n, whole, 0.0), axis=0, keepdims=True)
         totals[n : n + 1, :] = line[:, 0:M]
 
+    for f in range(F):
+        pltpu.make_async_copy(out.at[f], out_h.at[f], so.at[f]).wait()
     for c in tile_copies + copies + copies_x:
         c.wait_send()
     for (dx, dy), c in disp_moves:
@@ -374,7 +402,14 @@
     wide = -(-max(3 * TILE, ngy * cap) // TILE) * TILE
     vmem, dma = pltpu.VMEM, pltpu.SemaphoreType.DMA
     spec = pl.BlockSpec(memory_space=pltpu.VMEM)
+    far = pl.BlockSpec(memory_space=pltpu.HBM)
+    inputs = (density, energy, displacement, tile_mat.T, store_frac, store_state, store_route)
     scratch = [
+        vmem((F, rows, width), f32),
+        dma((F,)),
+        *(vmem(x.shape, x.dtype) for x in inputs),
+        dma((7,)),
+        vmem((rows * (width // TILE), TILE), f32),
         vmem((ngy, cap + 8, wide), f32),
         vmem((ngy, cap + 8, wide), f32),
         vmem((8, width), f32),
@@ -401,13 +436,13 @@
     remapped, totals = pl.pallas_call(
         functools.partial(kernel, ngx, ngy, cap),
         out_shape=(jax.ShapeDtypeStruct((F, rows, width), f32), jax.ShapeDtypeStruct((2, M), f32)),
-        in_specs=[spec] * 7,
-        out_specs=(spec, spec),
+        in_specs=[far] * 7,
+        out_specs=(far, spec),
         scratch_shapes=scratch,
         compiler_params=pltpu.CompilerParams(
-            collective_id=0, has_side_effects=True, vmem_limit_bytes=40 * 1024 * 1024
+            collective_id=0, has_side_effects=True, vmem_limit_bytes=63 * 1024 * 1024
         ),
-    )(density, energy, displacement, tile_mat, store_frac, store_state, store_route)
+    )(*inputs)
     return remapped.reshape(M, 3, rows, width), totals
 
 

time: 34.8 us -> 31.3 us (0.90)
  local copies, waits for them, and re-layouts: 7.39 us -> 3.24 us
  Pallas kernels: 26.4 us -> 27.3 us
    unnamed x15 -> x4, local copies, waits for them, and re-layouts: 7.39 us -> 3.24 us
    pallas_call x1, Pallas kernels: 26.4 us -> 27.3 us  [local(): pl.pallas_call(functools.partial(kernel, ngx, ngy, cap), out_shape=(jax.S...]
where the time goes in v2:
time: 31.3 us; the launch traced here: 31.2 us
  Pallas kernels  27.3 us (87%)
  local copies, waits for them, and re-layouts  3.24 us (10%)
  between operations  0.65 us (2%)
    pallas_call x1, Pallas kernels, local(): pl.pallas_call(functools.partial(kernel, ngx, ngy, cap), out_shape=(jax.S...  27.3 us
    unnamed x4, local copies, waits for them, and re-layouts  3.24 us

profile of v2, /device:TPU:0, one launch (start us, length us, event | category | flops | bytes accessed | tf_op | source)
XLA Modules:
  0.0 31.2 jit_solution(8924487924970471957)
XLA Ops:
  0.6 27.3 %shard_map.86 = (f32[12,64,512]{2,1,0:T(8,128)}, f32[2,4]{1,0:T(2,128)}) custom-call(f32[64,512]{1,0:T(8,128)} %density_h.1, f32[64,512]{1,0:T(8,128)} %energy_h.1, f32[2,64,512]{2,1,0:T(8,128)} %disp_h.1, s32[4,64]{1,0:T(4,128)} %bitcast.3, f32[32,128]{1,0:T(8,128)} %frac_h.1, f32[2,32,128]{2,1,0:T(8,128)} %state_h.1, s32[3,32]{1,0:T(4,128)} %route_h.1), custom_call_target="tpu_custom_call" | custom-call | tf_op jit(solution)/shard_map/pallas_call | solution.py:436
  27.9 0.0 copy-start
  27.9 2.7 %copy.11 = f32[4,3,64,512]{3,2,1,0:T(8,128)} copy(f32[4,3,64,512]{3,2,1,0:T(8,128)} %bitcast.2) | data formatting | bytes 3145728
  30.6 0.0 copy-done
  30.6 0.6 %copy.12 = f32[2,4]{1,0:T(2,128)} copy(f32[2,4]{1,0:T(2,128)S(1)} %copy-done) | data formatting | bytes 64
Async XLA Ops:
  27.9 2.7 %copy-start = (f32[2,4]{1,0:T(2,128)S(1)}, f32[2,4]{1,0:T(2,128)}, u32[]{:S(2)}) copy-start(f32[2,4]{1,0:T(2,128)} %get-tuple-element.9) | copy-start | bytes 100

commit v3 on v2

--- a/solution.py
+++ b/solution.py
@@ -38,8 +38,8 @@
 def kernel(
     ngx, ngy, cap,
     density_h, energy_h, disp_h, mat_h, frac_h, state_h, route_h,
-    out_h, totals,
-    out, so, density, energy, disp, mat, frac, state, route, s0,
+    out, totals,
+    density, energy, disp, mat, frac, state, route, s0,
     primary, send1, got1, drow, drow_in, dcol, dcol_in, de, ax, bx, ay, by,
     q, pk, xs, cols_in, rows_in, part, tot_y, tot_x, tot_sum,
     s1, r1, s2, r2, s3, r3, sy, ry, sx, rx,
@@ -333,7 +333,6 @@
         for c in range(1, per_row):
             lanes = lanes + total[:, c * TILE : (c + 1) * TILE]
         part[f] = lanes
-        pltpu.make_async_copy(out.at[f], out_h.at[f], so.at[f]).start()
         return carry
 
     lax.fori_loop(0, F, one_field, 0)
@@ -381,8 +380,6 @@
         line = jnp.sum(jnp.where(r8 == 2 * l8 + n, whole, 0.0), axis=0, keepdims=True)
         totals[n : n + 1, :] = line[:, 0:M]
 
-    for f in range(F):
-        pltpu.make_async_copy(out.at[f], out_h.at[f], so.at[f]).wait()
     for c in tile_copies + copies + copies_x:
         c.wait_send()
     for (dx, dy), c in disp_moves:
@@ -405,8 +402,6 @@
     far = pl.BlockSpec(memory_space=pltpu.HBM)
     inputs = (density, energy, displacement, tile_mat.T, store_frac, store_state, store_route)
     scratch = [
-        vmem((F, rows, width), f32),
-        dma((F,)),
         *(vmem(x.shape, x.dtype) for x in inputs),
         dma((7,)),
         vmem((rows * (width // TILE), TILE), f32),
@@ -435,12 +430,12 @@
     ]
     remapped, totals = pl.pallas_call(
         functools.partial(kernel, ngx, ngy, cap),
-        out_shape=(jax.ShapeDtypeStruct((F, rows, width), f32), jax.ShapeDtypeStruct((2, M), f32)),
+        out_shape=(pltpu.VMEM((F, rows, width), f32), jax.ShapeDtypeStruct((2, M), f32)),
         in_specs=[far] * 7,
-        out_specs=(far, spec),
+        out_specs=(spec, spec),
         scratch_shapes=scratch,
         compiler_params=pltpu.CompilerParams(
-            collective_id=0, has_side_effects=True, vmem_limit_bytes=63 * 1024 * 1024
+            collective_id=0, has_side_effects=True, vmem_limit_bytes=61 * 1024 * 1024
         ),
     )(*inputs)
     return remapped.reshape(M, 3, rows, width), totals

time: 31.3 us -> 29.7 us (0.949)
  local copies, waits for them, and re-layouts: 3.24 us -> 1.71 us
    unnamed x4, local copies, waits for them, and re-layouts: 3.24 us -> 1.71 us
where the time goes in v3:
time: 29.7 us; the launch traced here: 29.5 us
  Pallas kernels  27.1 us (91%)
  local copies, waits for them, and re-layouts  1.71 us (6%)
  between operations  0.65 us (2%)
    pallas_call x1, Pallas kernels, local(): pl.pallas_call(functools.partial(kernel, ngx, ngy, cap), out_shape=(pltpu...  27.1 us
    unnamed x4, local copies, waits for them, and re-layouts  1.71 us

profile of v3, /device:TPU:0, one launch (start us, length us, event | category | flops | bytes accessed | tf_op | source)
XLA Modules:
  0.0 29.5 jit_solution(1730079521827094145)
XLA Ops:
  0.6 27.1 %shard_map.86 = (f32[12,64,512]{2,1,0:T(8,128)S(1)}, f32[2,4]{1,0:T(2,128)}) custom-call(f32[64,512]{1,0:T(8,128)} %density_h.1, f32[64,512]{1,0:T(8,128)} %energy_h.1, f32[2,64,512]{2,1,0:T(8,128)} %disp_h.1, s32[4,64]{1,0:T(4,128)} %bitcast.3, f32[32,128]{1,0:T(8,128)} %frac_h.1, f32[2,32,128]{2,1,0:T(8,128)} %state_h.1, s32[3,32]{1,0:T(4,128)} %route_h.1), custom_call_target="tpu_custom_call" | custom-call | tf_op jit(solution)/shard_map/pallas_call | solution.py:431
  27.8 0.0 copy-start
  27.8 1.1 %copy.11 = f32[4,3,64,512]{3,2,1,0:T(8,128)} copy(f32[4,3,64,512]{3,2,1,0:T(8,128)S(1)} %bitcast.2) | data formatting | bytes 3145728
  28.9 0.0 copy-done
  28.9 0.6 %copy.12 = f32[2,4]{1,0:T(2,128)} copy(f32[2,4]{1,0:T(2,128)S(1)} %copy-done) | data formatting | bytes 64
Async XLA Ops:
  27.8 1.2 %copy-start = (f32[2,4]{1,0:T(2,128)S(1)}, f32[2,4]{1,0:T(2,128)}, u32[]{:S(2)}) copy-start(f32[2,4]{1,0:T(2,128)} %get-tuple-element.11) | copy-start | bytes 100

commit v4 on v3

--- a/solution.py
+++ b/solution.py
@@ -19,20 +19,17 @@
     return lax.broadcasted_iota(jnp.int32, shape, dim)
 
 
-def split3(x):
+def split2(x):
     hi = x.astype(bf16)
     rest = x - hi.astype(f32)
-    mid = rest.astype(bf16)
-    low = (rest - mid.astype(f32)).astype(bf16)
-    return hi, mid, low
+    return hi, rest.astype(bf16)
 
 
 def pick(onehot, data):
-    parts = split3(data)
+    parts = split2(data)
     o = onehot.astype(bf16)
-    total = jnp.dot(o, parts[2], preferred_element_type=f32)
-    total = total + jnp.dot(o, parts[1], preferred_element_type=f32)
-    return total + jnp.dot(o, parts[0], preferred_element_type=f32)
+    low = jnp.dot(o, parts[1], preferred_element_type=f32)
+    return low + jnp.dot(o, parts[0], preferred_element_type=f32)
 
 
 def kernel(
@@ -71,7 +68,7 @@
             )
         )
     ]
-    for c in loads:
+    for c in loads[:3]:
         c.start()
 
     barrier = pltpu.get_barrier_semaphore()
@@ -84,6 +81,9 @@
         @pl.when(exists(dx, dy))
         def _(dx=dx, dy=dy):
             pl.semaphore_signal(barrier, inc=1, device_id=(gx + dx, gy + dy), device_id_type=MESH)
+
+    for c in loads[3:]:
+        c.start()
 
     count = ngy * cap
     loads[0].wait()
@@ -99,11 +99,13 @@
     payload = jnp.concatenate([frac[...], state[0], state[1]], axis=1)
     packed = pick(chosen, payload)
     named = jnp.concatenate(
-        [(route[1:3, :] + 1).astype(f32), jnp.zeros((6, slots), f32)], axis=0
-    )
-    labels = lax.dot_general(
-        named, chosen, NT, precision=lax.Precision.HIGHEST, preferred_element_type=f32
-    )
+        [
+            ((route[1:2, :] + 1) // 128).astype(f32), (route[2:3, :] + 1).astype(f32),
+            ((route[1:2, :] + 1) % 128).astype(f32), jnp.zeros((5, slots), f32),
+        ],
+        axis=0,
+    )
+    labels = lax.dot_general(named.astype(bf16), chosen.astype(bf16), NT, preferred_element_type=f32)
     label_lane = iota((8, count), 1) // cap
     wide = send1.shape[2]
     for k in range(ngy):
@@ -199,7 +201,8 @@
     tiles = per_row * rows
     place = iota((tiles, count), 0)
     place = (place % rows) * per_row + place // rows + 1
-    hit = (jnp.broadcast_to(label[0:1, :].astype(jnp.int32), (tiles, count)) == place).astype(f32)
+    tile_at = (label[0:1, :] * 128.0 + label[2:3, :]).astype(jnp.int32)
+    hit = (jnp.broadcast_to(tile_at, (tiles, count)) == place).astype(f32)
     arrived = jnp.concatenate([got1[k, 0:cap, 0 : 3 * TILE] for k in range(ngy)], axis=0)
     mixed = pick(hit, arrived)
     second = jnp.dot(
@@ -222,6 +225,13 @@
             oth = jnp.where(other_m == m + 1.0, fr, 0.0)
             for n, value in enumerate((own + oth, own * d1 + oth * d2, own * de1 + oth * de2)):
                 q[3 * m + n, 8 : 8 + rows, lanes] = value
+    for f in range(F):
+        xs[0, 2 * f : 2 * f + 2] = q[f, 8:16, 0:width][0:2]
+        xs[1, 2 * f : 2 * f + 2] = q[f, rows : rows + 8, 0:width][6:8]
+    for dx, dy, c in halo[6:]:
+        @pl.when(exists(dx, dy))
+        def _(c=c):
+            c.start()
     acc = jnp.zeros((rows, TILE), f32)
     for f in range(F):
         both = jnp.where(
@@ -230,13 +240,6 @@
         acc = jnp.where(lane_r // 4 == f, pltpu.roll(both, 4 * f + 2, 1), acc)
     pk[...] = acc
     for dx, dy, c in halo[:6]:
-        @pl.when(exists(dx, dy))
-        def _(c=c):
-            c.start()
-    for f in range(F):
-        xs[0, 2 * f : 2 * f + 2] = q[f, 8:16, 0:width][0:2]
-        xs[1, 2 * f : 2 * f + 2] = q[f, rows : rows + 8, 0:width][6:8]
-    for dx, dy, c in halo[6:]:
         @pl.when(exists(dx, dy))
         def _(c=c):
             c.start()

time: 29.7 us -> 29.6 us (level)
  no operation moved by 1% of the time
where the time goes in v4:
time: 29.6 us; the launch traced here: 29.5 us
  Pallas kernels  27.1 us (92%)
  local copies, waits for them, and re-layouts  1.71 us (6%)
  between operations  0.65 us (2%)
    pallas_call x1, Pallas kernels, local(): pl.pallas_call(functools.partial(kernel, ngx, ngy, cap), out_shape=(pltpu...  27.1 us
    unnamed x4, local copies, waits for them, and re-layouts  1.71 us

profile of v4, /device:TPU:0, one launch (start us, length us, event | category | flops | bytes accessed | tf_op | source)
XLA Modules:
  0.0 29.5 jit_solution(5432708332838835878)
XLA Ops:
  0.6 27.1 %shard_map.86 = (f32[12,64,512]{2,1,0:T(8,128)S(1)}, f32[2,4]{1,0:T(2,128)}) custom-call(f32[64,512]{1,0:T(8,128)} %density_h.1, f32[64,512]{1,0:T(8,128)} %energy_h.1, f32[2,64,512]{2,1,0:T(8,128)} %disp_h.1, s32[4,64]{1,0:T(4,128)} %bitcast.3, f32[32,128]{1,0:T(8,128)} %frac_h.1, f32[2,32,128]{2,1,0:T(8,128)} %state_h.1, s32[3,32]{1,0:T(4,128)} %route_h.1), custom_call_target="tpu_custom_call" | custom-call | tf_op jit(solution)/shard_map/pallas_call | solution.py:434
  27.7 0.0 copy-start
  27.7 1.1 %copy.11 = f32[4,3,64,512]{3,2,1,0:T(8,128)} copy(f32[4,3,64,512]{3,2,1,0:T(8,128)S(1)} %bitcast.2) | data formatting | bytes 3145728
  28.9 0.0 copy-done
  28.9 0.6 %copy.12 = f32[2,4]{1,0:T(2,128)} copy(f32[2,4]{1,0:T(2,128)S(1)} %copy-done) | data formatting | bytes 64
Async XLA Ops:
  27.7 1.2 %copy-start = (f32[2,4]{1,0:T(2,128)S(1)}, f32[2,4]{1,0:T(2,128)}, u32[]{:S(2)}) copy-start(f32[2,4]{1,0:T(2,128)} %get-tuple-element.11) | copy-start | bytes 100

commit v5 on v4

--- a/solution.py
+++ b/solution.py
@@ -338,7 +338,10 @@
         part[f] = lanes
         return carry
 
-    lax.fori_loop(0, F, one_field, 0)
+    def volumes(first, last):
+        lax.fori_loop(first, last, lambda m, carry: one_field(3 * m, carry), 0)
+
+    lax.fori_loop(0, 2 * M, lambda n, carry: one_field(n + n // 2 + 1, carry), 0)
 
     mine = jnp.concatenate(
         [jnp.sum(part[3 * m + n], axis=0, keepdims=True) for m in range(M) for n in (1, 2)], axis=0
@@ -350,6 +353,7 @@
     ]
     for c in copies:
         c.start()
+    volumes(0, M // 2)
     incoming = [
         remote(tot_y.at[lax.rem(gy + ngy - k, ngy)], tot_y.at[lax.rem(gy + ngy - k, ngy)], sy.at[k], ry.at[k],
                (gx, lax.rem(gy + k, ngy)))
@@ -367,6 +371,7 @@
     ]
     for c in copies_x:
         c.start()
+    volumes(M // 2, M)
     incoming = [
         remote(tot_x.at[lax.rem(gx + ngx - k, ngx)], tot_x.at[lax.rem(gx + ngx - k, ngx)], sx.at[k], rx.at[k],
                (lax.rem(gx + k, ngx), gy))

time: 29.6 us -> 27.9 us (0.943)
  Pallas kernels: 27.1 us -> 25.4 us
    pallas_call x1, Pallas kernels: 27.1 us -> 25.4 us  [local(): pl.pallas_call(functools.partial(kernel, ngx, ngy, cap), out_shape=(pltpu...]
where the time goes in v5:
time: 27.9 us; the launch traced here: 27.7 us
  Pallas kernels  25.4 us (91%)
  local copies, waits for them, and re-layouts  1.71 us (6%)
  between operations  0.65 us (2%)
    pallas_call x1, Pallas kernels, local(): pl.pallas_call(functools.partial(kernel, ngx, ngy, cap), out_shape=(pltpu...  25.4 us
    unnamed x4, local copies, waits for them, and re-layouts  1.71 us

profile of v5, /device:TPU:0, one launch (start us, length us, event | category | flops | bytes accessed | tf_op | source)
XLA Modules:
  0.0 27.7 jit_solution(10456604977742732868)
XLA Ops:
  0.6 25.4 %shard_map.86 = (f32[12,64,512]{2,1,0:T(8,128)S(1)}, f32[2,4]{1,0:T(2,128)}) custom-call(f32[64,512]{1,0:T(8,128)} %density_h.1, f32[64,512]{1,0:T(8,128)} %energy_h.1, f32[2,64,512]{2,1,0:T(8,128)} %disp_h.1, s32[4,64]{1,0:T(4,128)} %bitcast.3, f32[32,128]{1,0:T(8,128)} %frac_h.1, f32[2,32,128]{2,1,0:T(8,128)} %state_h.1, s32[3,32]{1,0:T(4,128)} %route_h.1), custom_call_target="tpu_custom_call" | custom-call | tf_op jit(solution)/shard_map/pallas_call | solution.py:439
  26.0 0.0 copy-start
  26.0 1.1 %copy.11 = f32[4,3,64,512]{3,2,1,0:T(8,128)} copy(f32[4,3,64,512]{3,2,1,0:T(8,128)S(1)} %bitcast.2) | data formatting | bytes 3145728
  27.2 0.0 copy-done
  27.2 0.6 %copy.12 = f32[2,4]{1,0:T(2,128)} copy(f32[2,4]{1,0:T(2,128)S(1)} %copy-done) | data formatting | bytes 64
Async XLA Ops:
  26.0 1.2 %copy-start = (f32[2,4]{1,0:T(2,128)S(1)}, f32[2,4]{1,0:T(2,128)}, u32[]{:S(2)}) copy-start(f32[2,4]{1,0:T(2,128)} %get-tuple-element.11) | copy-start | bytes 100
